TPU v7x, 32 devices: a whole 2x2x4 slice. The times are simulated.
32 devices in a mesh: fsdp: 32 (over z, y, x, core).
Axes of the slice: x: 2, y: 2, z: 4, core: 2. Of those that a mesh axis runs over, the one named last changes fastest.
Arguments:
- loop_state: bfloat16 [65536, 256], P('fsdp'), may hold values from -6 to 6
- embedding: bfloat16 [65536, 256], P('fsdp'), may hold values from -6 to 6
- output_grad: bfloat16 [65536, 256], P('fsdp'), may hold values from -6 to 6
- entry_weight: bfloat16 [256, 768], P('fsdp'), may hold values from -0.375 to 0.375
- exit_weight: bfloat16 [256, 256], P('fsdp'), may hold values from -1.5 to 1.5
- lead_gain: bfloat16 [256], P('fsdp'), may hold values from 0.25 to 1.75
- lead_shift: bfloat16 [256], P('fsdp'), may hold values from -3 to 3
- expand_weight: bfloat16 [256, 1024], P('fsdp'), may hold values from -0.375 to 0.375
- reduce_weight: bfloat16 [1024, 256], P('fsdp'), may hold values from -0.25 to 0.25
- middle_gain: bfloat16 [256], P('fsdp'), may hold values from 0.25 to 1.75
- middle_shift: bfloat16 [256], P('fsdp'), may hold values from -3 to 3
- expand_bias: bfloat16 [1024], P('fsdp'), may hold values from -3 to 3
- reduce_bias: bfloat16 [256], P('fsdp'), may hold values from -3 to 3
Outputs:
- final_state: bfloat16 [65536, 256], P('fsdp')
- state_grad: float32 [65536, 256], P('fsdp')
- embed_grad: float32 [65536, 256], P('fsdp')
- entry_grad: float32 [256, 768], P('fsdp')
- exit_grad: float32 [256, 256], P('fsdp')
- lead_gain_grad: float32 [256], P('fsdp')
- lead_shift_grad: float32 [256], P('fsdp')
- expand_grad: float32 [256, 1024], P('fsdp')
- reduce_grad: float32 [1024, 256], P('fsdp')
- middle_gain_grad: float32 [256], P('fsdp')
- middle_shift_grad: float32 [256], P('fsdp')
- expand_bias_grad: float32 [1024], P('fsdp')
- reduce_bias_grad: float32 [256], P('fsdp')
All inputs are finite; a program needn't handle non-finite values.
Results may differ from a plain program's by a relative error of at most 0.013.
Values may be sent and summed in bfloat16 or wider, within the bound.
A program may use at most 192 MiB of HBM per device.

v0:
```python
import jax
import jax.numpy as jnp
from jax import lax
from jax.sharding import PartitionSpec as P

LEN = 1024
LOOPS = 2


EPS = 1e-05


def norm_layer(values, gain, shift):
    center = values - jnp.mean(values, axis=-1, keepdims=True)
    spread = jnp.mean(center * center, axis=-1, keepdims=True)
    return center * lax.rsqrt(spread + EPS) * gain + shift


def norm_back(values, gain, shift, grad):
    result, pull = jax.vjp(norm_layer, values, gain, shift)
    return pull(grad)


def gelu_exact(values):
    return jax.nn.gelu(values, approximate=False)


def split_heads(qkv, width, heads):
    tokens = qkv.shape[0]
    seqs = tokens // LEN
    size = width // heads
    query = qkv[:, :width].reshape(seqs, LEN, heads, size)
    keys = qkv[:, width : 2 * width].reshape(seqs, LEN, heads, size)
    values = qkv[:, 2 * width :].reshape(seqs, LEN, heads, size)
    return (query, keys, values)


def attend_forward(qkv, width, heads):
    query, keys, values = split_heads(qkv, width, heads)
    block = min(512, LEN)
    key_place = jnp.arange(LEN)

    def one_block(index):
        start = index * block
        q_block = lax.dynamic_slice_in_dim(query, start, block, 1)
        scores = (
            jnp.einsum("sqhd,skhd->shqk", q_block, keys, preferred_element_type=jnp.float32) * 0.125
        )
        allowed = key_place[None, :] <= (start + jnp.arange(block))[:, None]
        scores = jnp.where(allowed, scores, -1e30)
        top = jnp.max(scores, axis=-1, keepdims=True)
        weights = jnp.exp(scores - top)
        total = jnp.sum(weights, axis=-1, keepdims=True)
        probs = (weights / total).astype(jnp.bfloat16)
        out_block = jnp.einsum("shqk,skhd->sqhd", probs, values, preferred_element_type=jnp.float32)
        return (out_block.astype(jnp.bfloat16), (top + jnp.log(total))[..., 0])

    blocks, logsum = lax.map(one_block, jnp.arange(LEN // block))
    attended = jnp.transpose(blocks, (1, 0, 2, 3, 4)).reshape(qkv.shape[0], width)
    return (attended, logsum)


def attend_backward(qkv, logsum, d_attended, width, heads):
    query, keys, values = split_heads(qkv, width, heads)
    seqs = query.shape[0]
    d_heads = d_attended.reshape(seqs, LEN, heads, width // heads)
    block = min(512, LEN)
    key_place = jnp.arange(LEN)

    def one_block(carry, index):
        d_keys, d_values = carry
        start = index * block
        q_block = lax.dynamic_slice_in_dim(query, start, block, 1)
        g_block = lax.dynamic_slice_in_dim(d_heads, start, block, 1)
        scores = (
            jnp.einsum("sqhd,skhd->shqk", q_block, keys, preferred_element_type=jnp.float32) * 0.125
        )
        allowed = key_place[None, :] <= (start + jnp.arange(block))[:, None]
        probs = jnp.where(allowed, jnp.exp(scores - logsum[index][..., None]), 0.0)
        d_probs = jnp.einsum("sqhd,skhd->shqk", g_block, values, preferred_element_type=jnp.float32)
        inner = jnp.sum(probs * d_probs, axis=-1, keepdims=True)
        d_scores = (probs * (d_probs - inner)).astype(jnp.bfloat16)
        d_query = (
            jnp.einsum("shqk,skhd->sqhd", d_scores, keys, preferred_element_type=jnp.float32)
            * 0.125
        )
        d_keys = (
            d_keys
            + jnp.einsum("shqk,sqhd->skhd", d_scores, q_block, preferred_element_type=jnp.float32)
            * 0.125
        )
        d_values = d_values + jnp.einsum(
            "shqk,sqhd->skhd",
            probs.astype(jnp.bfloat16),
            g_block,
            preferred_element_type=jnp.float32,
        )
        return ((d_keys, d_values), d_query)

    empty = jnp.zeros(query.shape, jnp.float32)
    carried, d_blocks = lax.scan(one_block, (empty, empty), jnp.arange(LEN // block))
    tokens = qkv.shape[0]
    d_query = jnp.transpose(d_blocks, (1, 0, 2, 3, 4)).reshape(tokens, width)
    joined = jnp.concatenate(
        [d_query, carried[0].reshape(tokens, width), carried[1].reshape(tokens, width)], axis=1
    )
    return joined.astype(jnp.bfloat16)


def forward_loop(state, embed, attend, feed):
    entry_w, exit_w, lead_g, lead_s = attend
    expand_w, reduce_w, mid_g, mid_s, expand_b, reduce_b = feed
    width = state.shape[1]
    heads = width // 64
    mixed = state + embed
    normed = norm_layer(mixed, lead_g.astype(jnp.float32), lead_s.astype(jnp.float32)).astype(
        jnp.bfloat16
    )
    qkv = jnp.dot(normed, entry_w, preferred_element_type=jnp.float32).astype(jnp.bfloat16)
    attended, logsum = attend_forward(qkv, width, heads)
    middle = mixed + jnp.dot(attended, exit_w, preferred_element_type=jnp.float32)
    normed2 = norm_layer(middle, mid_g.astype(jnp.float32), mid_s.astype(jnp.float32)).astype(
        jnp.bfloat16
    )
    hidden = jnp.dot(normed2, expand_w, preferred_element_type=jnp.float32) + expand_b.astype(
        jnp.float32
    )
    active = gelu_exact(hidden).astype(jnp.bfloat16)
    result = (
        middle
        + jnp.dot(active, reduce_w, preferred_element_type=jnp.float32)
        + reduce_b.astype(jnp.float32)
    )
    kept = (mixed, normed, qkv, attended, logsum, middle, normed2, hidden, active)
    return (result, kept)


def backward_loop(state, embed, attend, feed, grad):
    entry_w, exit_w, lead_g, lead_s = attend
    expand_w, reduce_w, mid_g, mid_s, expand_b, reduce_b = feed
    width = state.shape[1]
    heads = width // 64
    result, kept = forward_loop(state, embed, attend, feed)
    mixed, normed, qkv, attended, logsum, middle, normed2, hidden, active = kept
    d_out = grad.astype(jnp.bfloat16)
    g_reduce_b = jnp.sum(d_out.astype(jnp.float32), axis=0)
    g_reduce = jnp.einsum("ti,to->io", active, d_out, preferred_element_type=jnp.float32)
    d_active = jnp.einsum("to,io->ti", d_out, reduce_w, preferred_element_type=jnp.float32)
    hidden_out, gelu_pull = jax.vjp(gelu_exact, hidden)
    d_hidden = gelu_pull(d_active)[0].astype(jnp.bfloat16)
    g_expand_b = jnp.sum(d_hidden.astype(jnp.float32), axis=0)
    g_expand = jnp.einsum("ti,to->io", normed2, d_hidden, preferred_element_type=jnp.float32)
    d_normed2 = jnp.einsum("to,io->ti", d_hidden, expand_w, preferred_element_type=jnp.float32)
    d_mid_part, g_mid_g, g_mid_s = norm_back(
        middle, mid_g.astype(jnp.float32), mid_s.astype(jnp.float32), d_normed2
    )
    d_middle = grad + d_mid_part
    d_branch = d_middle.astype(jnp.bfloat16)
    g_exit = jnp.einsum("ti,to->io", attended, d_branch, preferred_element_type=jnp.float32)
    d_attended = jnp.einsum(
        "to,io->ti", d_branch, exit_w, preferred_element_type=jnp.float32
    ).astype(jnp.bfloat16)
    d_qkv = attend_backward(qkv, logsum, d_attended, width, heads)
    g_entry = jnp.einsum("ti,to->io", normed, d_qkv, preferred_element_type=jnp.float32)
    d_normed = jnp.einsum("to,io->ti", d_qkv, entry_w, preferred_element_type=jnp.float32)
    d_mix_part, g_lead_g, g_lead_s = norm_back(
        mixed, lead_g.astype(jnp.float32), lead_s.astype(jnp.float32), d_normed
    )
    d_mixed = d_middle + d_mix_part
    return (
        d_mixed,
        (g_entry, g_exit, g_lead_g, g_lead_s),
        (g_expand, g_reduce, g_mid_g, g_mid_s, g_expand_b, g_reduce_b),
    )


def add_terms(totals, terms):
    if totals is None:
        return terms
    return tuple((a + b for a, b in zip(totals, terms)))


def on_device(
    loop_state,
    embedding,
    output_grad,
    entry_weight,
    exit_weight,
    lead_gain,
    lead_shift,
    expand_weight,
    reduce_weight,
    middle_gain,
    middle_shift,
    expand_bias,
    reduce_bias,
):
    attend = (
        lax.all_gather(entry_weight, "fsdp", axis=0, tiled=True),
        lax.all_gather(exit_weight, "fsdp", axis=0, tiled=True),
        lax.all_gather(lead_gain, "fsdp", axis=0, tiled=True),
        lax.all_gather(lead_shift, "fsdp", axis=0, tiled=True),
    )
    feed = (
        lax.all_gather(expand_weight, "fsdp", axis=0, tiled=True),
        lax.all_gather(reduce_weight, "fsdp", axis=0, tiled=True),
        lax.all_gather(middle_gain, "fsdp", axis=0, tiled=True),
        lax.all_gather(middle_shift, "fsdp", axis=0, tiled=True),
        lax.all_gather(expand_bias, "fsdp", axis=0, tiled=True),
        lax.all_gather(reduce_bias, "fsdp", axis=0, tiled=True),
    )
    embed = embedding.astype(jnp.float32)
    state = loop_state.astype(jnp.float32)
    inputs = []
    for turn in range(LOOPS):
        inputs.append(state)
        state = forward_loop(state, embed, attend, feed)[0]
    final_state = state.astype(jnp.bfloat16)
    grad = output_grad.astype(jnp.float32)
    embed_total = jnp.zeros_like(embed)
    attend_total = None
    feed_total = None
    for turn in reversed(range(LOOPS)):
        grad, attend_terms, feed_terms = backward_loop(inputs[turn], embed, attend, feed, grad)
        embed_total = embed_total + grad
        attend_total = add_terms(attend_total, attend_terms)
        feed_total = add_terms(feed_total, feed_terms)
    attend_total = lax.psum_scatter(attend_total, "fsdp", scatter_dimension=0, tiled=True)
    feed_total = lax.psum_scatter(feed_total, "fsdp", scatter_dimension=0, tiled=True)
    return (
        final_state,
        grad,
        embed_total,
        attend_total[0],
        attend_total[1],
        attend_total[2],
        attend_total[3],
        feed_total[0],
        feed_total[1],
        feed_total[2],
        feed_total[3],
        feed_total[4],
        feed_total[5],
    )


def solution(mesh):
    in_specs = (
        P("fsdp", None),
        P("fsdp", None),
        P("fsdp", None),
        P("fsdp", None),
        P("fsdp", None),
        P("fsdp"),
        P("fsdp"),
        P("fsdp", None),
        P("fsdp", None),
        P("fsdp"),
        P("fsdp"),
        P("fsdp"),
        P("fsdp"),
    )
    out_specs = (
        P("fsdp", None),
        P("fsdp", None),
        P("fsdp", None),
        P("fsdp", None),
        P("fsdp", None),
        P("fsdp"),
        P("fsdp"),
        P("fsdp", None),
        P("fsdp", None),
        P("fsdp"),
        P("fsdp"),
        P("fsdp"),
        P("fsdp"),
    )
    return jax.shard_map(
        on_device, mesh=mesh, in_specs=in_specs, out_specs=out_specs, check_vma=False
    )
```

profile of v0, /device:TPU:0, one launch (start us, length us, event | category | flops | bytes accessed | tf_op | source)
XLA Modules:
  0.0 1159.4 jit_solution(10424568494132584494)
XLA Ops:
  12.4 42.1 %all-reduce.13 = (bf16[256]{0:T(256)(128)(2,1)S(1)}, bf16[256]{0:T(256)(128)(2,1)S(1)}, bf16[1024]{0:T(1024)(128)(2,1)S(1)}, bf16[256]{0:T(256)(128)(2,1)S(1)}, ...) all-reduce(bf16[256]{0:T(256)(128)(2,1)S(1)} %dynamic-update-slice.1, ...), channel_id=1, replica_groups=mesh['fsdp'=32] {'fsdp'}, use_global_device_ids=true, to_apply=%add.1 | all-reduce | flops 2304 | bytes 9216
  57.9 43.4 %all_gather.33 = bf16[256,256]{1,0:T(8,128)(2,1)} all-gather(bf16[8,256]{1,0:T(8,128)(2,1)} %param.29), channel_id=1, replica_groups=mesh['fsdp'=32] {'fsdp'}, dimensions={0}, use_global_device_ids=true | all-gather | bytes 135168 | tf_op jit(solution)/shard_map/all_gather | solution.py:200
  101.3 37.9 %all_gather.32 = bf16[256,768]{1,0:T(8,128)(2,1)S(1)} all-gather(bf16[8,768]{1,0:T(8,128)(2,1)} %param.28), channel_id=1, replica_groups=mesh['fsdp'=32] {'fsdp'}, dimensions={0}, use_global_device_ids=true | all-gather | bytes 405504 | tf_op jit(solution)/shard_map/all_gather | solution.py:199
  139.2 42.3 %all_gather.36 = bf16[256,1024]{1,0:T(8,128)(2,1)} all-gather(bf16[8,1024]{1,0:T(8,128)(2,1)} %param.32), channel_id=1, replica_groups=mesh['fsdp'=32] {'fsdp'}, dimensions={0}, use_global_device_ids=true | all-gather | bytes 540672 | tf_op jit(solution)/shard_map/all_gather | solution.py:205
  181.5 40.9 %all_gather.38 = bf16[1024,256]{1,0:T(8,128)(2,1)} all-gather(bf16[32,256]{1,0:T(8,128)(2,1)} %param.33), channel_id=1, replica_groups=mesh['fsdp'=32] {'fsdp'}, dimensions={0}, use_global_device_ids=true | all-gather | bytes 540672 | tf_op jit(solution)/shard_map/all_gather | solution.py:206
  250.3 30.9 %while.81 = (s32[]{:T(128)}, bf16[2,2,512,4,64]{2,4,3,1,0:T(8,128)(2,1)}, f32[2,2,4,512]{3,2,1,0:T(4,128)S(1)}, s32[2]{0:T(128)S(1)}, bf16[2,1024,4,64]{1,3,2,0:...) while((s32[]{:T(128)}, ...), condition=%wide.region_32.33_spmd.clone, body=%wide.region_29.32_spmd.clone.sunk | while | flops 1124856320 | bytes 64098548 | solution.py:58
  288.6 44.6 %while.78 = (s32[]{:T(128)}, bf16[2,2,512,4,64]{2,4,3,1,0:T(8,128)(2,1)}, s32[2]{0:T(128)S(1)}, bf16[2,1024,4,64]{1,3,2,0:T(8,128)(2,1)S(1)}, bf16[2,1024,4,64]{...) while((s32[]{:T(128)}, ...), condition=%wide.region_5.6_spmd.clone, body=%wide.region_2.5_spmd.clone.sunk | while | flops 1099695616 | bytes 37785776 | solution.py:58
  291.1 10.3 fusion.388
  313.3 10.3 fusion.388
  343.7 23.1 %fusion.274 = (f32[2048]{0:T(1024)S(1)}, f32[2048,256]{0,1:T(8,128)S(1)}) fusion(bf16[2048,256]{0,1:T(8,128)(2,1)} %copy-done.18, f32[256]{0:T(256)S(1)} %copy-done.137, f32[2048,256]{0,1:T(8,128)} %copy-done.49, bf16[1024,256]{1,0:T(8,128)(2,1)} %all_gather.38, bf16[256,1024]{1,0:T(8,128)(2,1)} %all_gather.36, f32[1024]{0:T(1024)S(1)} %copy-done.86, ...), kind=kOutput, calls=%fused_computation.387 | convolution fusion | flops 2291136512 | bytes 6323200 | tf_op jit(solution)/shard_map/dot_general | solution.py:131
  393.5 33.2 %while.80 = (s32[]{:T(128)}, bf16[2,2,512,4,64]{2,4,3,1,0:T(8,128)(2,1)}, f32[2,2,4,512]{3,2,1,0:T(4,128)S(1)}, s32[2]{0:T(128)S(1)}, bf16[2,1024,4,64]{1,3,2,0:...) while((s32[]{:T(128)}, ...), condition=%wide.region_19.20_spmd.clone, body=%wide.region_16.19_spmd.clone.sunk | while | flops 1124856320 | bytes 68292880 | solution.py:58
  438.6 40.4 %fusion.129 = (f32[2048,1024]{1,0:T(8,128)}, f32[2048,1024]{1,0:T(8,128)S(1)}, f32[2048,1024]{1,0:T(8,128)}) fusion(f32[1024]{0:T(1024)S(1)} %copy-done.87, f32[2048,1024]{1,0:T(8,128)S(1)} %fusion.255, bf16[256,1024]{1,0:T(8,128)(2,1)S(1)} %copy-done.69, f32[2048,256]{0,1:T(8,128)S(1)} %copy-done.32, f32[2048]{0:T(1024)S(1)} %copy-done.97, ...), kind=kOutput, calls=%fused_computation.147 | convolution fusion | flops 1340604416 | bytes 36198400 | tf_op jit(solution)/shard_map/dot_general | solution.py:125
  506.7 94.4 %while.82 = (s32[]{:T(128)}, f32[2,1024,4,64]{1,3,2,0:T(8,128)}, f32[2,1024,4,64]{1,3,2,0:T(8,128)}, bf16[2,2,512,4,64]{2,4,3,1,0:T(8,128)(2,1)}, s32[2]{0:T(128...) while((s32[]{:T(128)}, f32[2,1024,4,64]{1,3,2,0:T(8,128)}, ...), condition=%wide.region_26.27_spmd.clone, body=%wide.region_24.26_spmd.clone.sunk | while | flops 2750673408 | bytes 199676400 | solution.py:101
  519.5 11.6 %multiply_reduce_fusion.18 = (f32[2,4,512]{2,1,0:T(4,128)}, f32[2,4,512,1024]{3,2,1,0:T(8,128)}) fusion(f32[2,4,512,1024]{3,2,1,0:T(8,128)S(1)} %fusion.414, f32[2,4,512]{2,1,0:T(4,128)} %copy-done.67, pred[512,1024]{1,0:T(8,128)(4,1)} %copy-done.6, bf16[2,1024,4,64]{1,3,2,0:T(8,128)(2,1)} %get-tuple-element.1245, ...), kind=kOutput, calls=%fused_computation.85.clone.1 | convolution fusion | flops 557838336 | bytes 35684356 | tf_op jit(solution)/shard_map/while/body/eval_jaxpr/sqhd,skhd->shqk/dot_general | solution.py:80
  531.1 11.0 multiply_convert_fusion.10
  567.0 11.6 %multiply_reduce_fusion.18 = (f32[2,4,512]{2,1,0:T(4,128)}, f32[2,4,512,1024]{3,2,1,0:T(8,128)}) fusion(f32[2,4,512,1024]{3,2,1,0:T(8,128)S(1)} %fusion.414, f32[2,4,512]{2,1,0:T(4,128)} %copy-done.67, pred[512,1024]{1,0:T(8,128)(4,1)} %copy-done.6, bf16[2,1024,4,64]{1,3,2,0:T(8,128)(2,1)} %get-tuple-element.1245, ...), kind=kOutput, calls=%fused_computation.85.clone.1 | convolution fusion | flops 557838336 | bytes 35684356 | tf_op jit(solution)/shard_map/while/body/eval_jaxpr/sqhd,skhd->shqk/dot_general | solution.py:80
  578.6 11.0 multiply_convert_fusion.10
  627.3 9.8 convert_reduce_fusion
  666.7 95.9 %while.83 = (s32[]{:T(128)}, f32[2,1024,4,64]{1,3,2,0:T(8,128)}, f32[2,1024,4,64]{1,3,2,0:T(8,128)}, bf16[2,2,512,4,64]{2,4,3,1,0:T(8,128)(2,1)}, s32[2]{0:T(128...) while((s32[]{:T(128)}, f32[2,1024,4,64]{1,3,2,0:T(8,128)}, ...), condition=%wide.region_39.40_spmd.clone, body=%wide.region_37.39_spmd.clone.sunk | while | flops 2750673408 | bytes 199414192 | solution.py:101
  680.2 11.6 %multiply_reduce_fusion.19 = (f32[2,4,512]{2,1,0:T(4,128)}, f32[2,4,512,1024]{3,2,1,0:T(8,128)}) fusion(f32[2,4,512,1024]{3,2,1,0:T(8,128)S(1)} %fusion.425, f32[2,4,512]{2,1,0:T(4,128)} %copy-done.68, pred[512,1024]{1,0:T(8,128)(4,1)} %copy-done.7, bf16[2,1024,4,64]{1,3,2,0:T(8,128)(2,1)} %get-tuple-element.1290, ...), kind=kOutput, calls=%fused_computation.111.clone.1 | convolution fusion | flops 557838336 | bytes 35684356 | tf_op jit(solution)/shard_map/while/body/eval_jaxpr/sqhd,skhd->shqk/dot_general | solution.py:80
  691.8 11.1 multiply_convert_fusion.11
  728.5 11.6 %multiply_reduce_fusion.19 = (f32[2,4,512]{2,1,0:T(4,128)}, f32[2,4,512,1024]{3,2,1,0:T(8,128)}) fusion(f32[2,4,512,1024]{3,2,1,0:T(8,128)S(1)} %fusion.425, f32[2,4,512]{2,1,0:T(4,128)} %copy-done.68, pred[512,1024]{1,0:T(8,128)(4,1)} %copy-done.7, bf16[2,1024,4,64]{1,3,2,0:T(8,128)(2,1)} %get-tuple-element.1290, ...), kind=kOutput, calls=%fused_computation.111.clone.1 | convolution fusion | flops 557838336 | bytes 35684356 | tf_op jit(solution)/shard_map/while/body/eval_jaxpr/sqhd,skhd->shqk/dot_general | solution.py:80
  740.1 11.1 multiply_convert_fusion.11
  802.1 45.1 %while.79 = (s32[]{:T(128)}, bf16[2,2,512,4,64]{2,4,3,1,0:T(8,128)(2,1)}, s32[2]{0:T(128)S(1)}, bf16[2,1024,4,64]{1,3,2,0:T(8,128)(2,1)}, bf16[2,1024,4,64]{1,3,...) while((s32[]{:T(128)}, ...), condition=%wide.region_13.14_spmd.clone, body=%wide.region_10.13_spmd.clone.sunk | while | flops 1099695616 | bytes 37785776 | solution.py:58
  804.6 10.4 fusion.393
  815.0 9.7 fusion.394
  827.1 10.4 fusion.393
  837.5 9.6 fusion.394
  854.8 22.8 %fusion.162 = bf16[2048,256]{0,1:T(8,128)(2,1)S(1)} fusion(f32[2048,256]{0,1:T(8,128)} %copy-done.48, bf16[1024,256]{1,0:T(8,128)(2,1)} %all_gather.38, bf16[256,1024]{1,0:T(8,128)(2,1)} %all_gather.36, f32[1024]{0:T(1024)S(1)} %copy-done.89, f32[2048]{0:T(1024)S(1)} %add_rsqrt_fusion, f32[2048]{0:T(1024)S(1)} %broadcast_multiply_fusion.2, ...), kind=kOutput, calls=%fused_computation.234 | convolution fusion | flops 2290089984 | bytes 4217856 | tf_op jit(solution)/shard_map/dot_general | solution.py:131
  891.3 37.3 %all-reduce.12 = (f32[256]{0:T(256)S(1)}, f32[256]{0:T(256)S(1)}, f32[256]{0:T(256)S(1)}, f32[256]{0:T(256)S(1)}, f32[1024]{0:T(1024)S(1)}, /*index=5*/f32[256]{0:T(256)S(1)}) all-reduce(f32[256]{0:T(256)S(1)} %add.424, f32[256]{0:T(256)S(1)} %add.425, f32[256]{0:T(256)S(1)} %add.428, ...), channel_id=4, replica_groups=mesh['fsdp'=32] {'fsdp'}, use_global_device_ids=true, to_apply=%region_46.47.clone | all-reduce | flops 2304 | bytes 18432
  944.1 75.0 %reduce-scatter.9.cloned.1.call-done = f32[8,1024]{1,0:T(8,128)} async-done(((f32[256,1024]{1,0:T(8,128)}), f32[8,1024]{1,0:T(8,128)}) %reduce-scatter.9.cloned.1.call-update) | async-done | bytes 32784 | tf_op jit(solution)/shard_map/reduce_scatter | solution.py:229
  1019.1 133.6 %reduce-scatter.11.cloned.1.call-done = f32[32,256]{1,0:T(8,128)} async-done(((f32[1024,256]{1,0:T(8,128)}), f32[32,256]{1,0:T(8,128)}) %reduce-scatter.11.cloned.1.call-update) | async-done | bytes 32784 | tf_op jit(solution)/shard_map/reduce_scatter | solution.py:229
  (575 shorter events, 425.6 us)
Async XLA Ops:
  7.2 220.1 %copy-start.60 = (bf16[2048,256]{1,0:T(8,128)(2,1)S(1)}, bf16[2048,256]{1,0:T(8,128)(2,1)}, u32[]{:S(2)}) copy-start(bf16[2048,256]{1,0:T(8,128)(2,1)} %param.27) | copy-start | bytes 3145732
  7.2 936.9 %reduce-scatter.7.cloned.1.call-start = ((), (), s32[]{:S(2)}) async-start(), calls=%async_computation.5 | async-start | bytes 270336 | tf_op jit(solution)/shard_map/reduce_scatter | solution.py:228
  139.2 91.6 %copy-start.56 = (bf16[256,768]{1,0:T(8,128)(2,1)}, bf16[256,768]{1,0:T(8,128)(2,1)S(1)}, u32[]{:S(2)}) copy-start(bf16[256,768]{1,0:T(8,128)(2,1)S(1)} %all_gather.32) | copy-start | bytes 1179652
  288.6 51.6 %copy-start.19 = (bf16[2048,256]{0,1:T(8,128)(2,1)S(1)}, bf16[2048,256]{0,1:T(8,128)(2,1)}, u32[]{:S(2)}) copy-start(bf16[2048,256]{0,1:T(8,128)(2,1)} %copy-done.18) | copy-start | bytes 3145732
  288.6 51.6 %copy-start.52 = (bf16[256,256]{1,0:T(8,128)(2,1)S(1)}, bf16[256,256]{1,0:T(8,128)(2,1)}, u32[]{:S(2)}) copy-start(bf16[256,256]{1,0:T(8,128)(2,1)} %all_gather.33) | copy-start | bytes 393220
  333.2 33.7 %copy-start.2 = (bf16[2,1024,4,64]{1,3,2,0:T(8,128)(2,1)}, bf16[2,1024,4,64]{1,3,2,0:T(8,128)(2,1)S(1)}, u32[]{:S(2)}) copy-start(bf16[2,1024,4,64]{1,3,2,0:T(8,128)(2,1)S(1)} %get-tuple-element.1301) | copy-start | bytes 3145732
  333.2 10.5 copy-start.86
  333.2 10.5 copy-start.117
  333.2 10.5 copy-start.121
  333.2 10.5 copy-start.137
  393.4 39.2 %copy-start.13 = (f32[2048,256]{0,1:T(8,128)S(1)}, f32[2048,256]{0,1:T(8,128)}, u32[]{:S(2)}) copy-start(f32[2048,256]{0,1:T(8,128)} %copy-done.12) | copy-start | bytes 6291460
  393.4 39.2 %copy-start.53 = (bf16[256,256]{1,0:T(8,128)(2,1)S(1)}, bf16[256,256]{1,0:T(8,128)(2,1)}, u32[]{:S(2)}) copy-start(bf16[256,256]{1,0:T(8,128)(2,1)} %all_gather.33) | copy-start | bytes 393220
  434.4 59.0 %copy-start.74 = (f32[2048]{0:T(1024)}, f32[2048]{0:T(1024)S(1)}, u32[]{:S(2)}) copy-start(f32[2048]{0:T(1024)S(1)} %broadcast_multiply_fusion.1) | copy-start | bytes 24580
  435.7 57.6 %copy-start.79 = (f32[2048]{0:T(1024)}, f32[2048]{0:T(1024)S(1)}, u32[]{:S(2)}) copy-start(f32[2048]{0:T(1024)S(1)} %fusion.186) | copy-start | bytes 24580
  438.6 40.5 %copy-start.16 = (f32[2048,1024]{1,0:T(8,128)}, f32[2048,1024]{1,0:T(8,128)S(1)}, u32[]{:S(2)}) copy-start(f32[2048,1024]{1,0:T(8,128)S(1)} %fusion.255) | copy-start | bytes 25165828
  438.6 40.5 %copy-start.61 = (bf16[2048,256]{1,0:T(8,128)(2,1)S(1)}, bf16[2048,256]{1,0:T(8,128)(2,1)}, u32[]{:S(2)}) copy-start(bf16[2048,256]{1,0:T(8,128)(2,1)} %param.27) | copy-start | bytes 3145732
  438.6 40.4 %copy-start.72 = (bf16[1024,256]{1,0:T(8,128)(2,1)S(1)}, bf16[1024,256]{1,0:T(8,128)(2,1)}, u32[]{:S(2)}) copy-start(bf16[1024,256]{1,0:T(8,128)(2,1)} %all_gather.38) | copy-start | bytes 1572868
  495.5 11.1 copy-start.100
  601.1 10.4 copy-start.4
  613.7 11.7 %copy-start.45 = (bf16[2048,256]{0,1:T(8,128)(2,1)S(1)}, bf16[2048,256]{0,1:T(8,128)(2,1)}, u32[]{:S(2)}) copy-start(bf16[2048,256]{0,1:T(8,128)(2,1)} %copy.131) | copy-start | bytes 3145732
  613.7 11.7 %copy-start.101 = (f32[2048]{0:T(1024)S(1)}, f32[2048]{0:T(1024)}, u32[]{:S(2)}) copy-start(f32[2048]{0:T(1024)} %copy-done.100) | copy-start | bytes 24580
  653.2 291.0 %reduce-scatter.5.cloned.1.call-start = ((), (), s32[]{:S(2)}) async-start(), calls=%async_computation.4 | async-start | bytes 811008 | tf_op jit(solution)/shard_map/reduce_scatter | solution.py:228
  653.2 13.5 %copy-start.3 = (bf16[2,1024,4,64]{1,3,2,0:T(8,128)(2,1)S(1)}, bf16[2,1024,4,64]{1,3,2,0:T(8,128)(2,1)}, u32[]{:S(2)}) copy-start(bf16[2,1024,4,64]{1,3,2,0:T(8,128)(2,1)} %copy-done.2) | copy-start | bytes 3145732
  776.7 242.4 %reduce-scatter.9.cloned.1.call-start = ((), (), s32[]{:S(2)}) async-start(), calls=%async_computation.6 | async-start | bytes 1081344 | tf_op jit(solution)/shard_map/reduce_scatter | solution.py:229
  783.2 369.4 %reduce-scatter.11.cloned.1.call-start = ((), (), s32[]{:S(2)}) async-start(), calls=%async_computation.7 | async-start | bytes 1081344 | tf_op jit(solution)/shard_map/reduce_scatter | solution.py:229
  791.8 10.3 copy-start.5
  802.1 49.4 %copy-start.15 = (f32[2048,256]{0,1:T(8,128)S(1)}, f32[2048,256]{0,1:T(8,128)}, u32[]{:S(2)}) copy-start(f32[2048,256]{0,1:T(8,128)} %copy-done.12) | copy-start | bytes 6291460
  802.1 49.4 %copy-start.55 = (bf16[256,256]{1,0:T(8,128)(2,1)S(1)}, bf16[256,256]{1,0:T(8,128)(2,1)}, u32[]{:S(2)}) copy-start(bf16[256,256]{1,0:T(8,128)(2,1)} %all_gather.33) | copy-start | bytes 393220
  854.8 24.1 %copy-start.59 = (bf16[256,768]{1,0:T(8,128)(2,1)S(1)}, bf16[256,768]{1,0:T(8,128)(2,1)}, u32[]{:S(2)}) copy-start(bf16[256,768]{1,0:T(8,128)(2,1)} %copy-done.56) | copy-start | bytes 1179652
  877.6 11.1 copy-start.103
  879.0 12.3 %copy-start.130 = (f32[256]{0:T(256)S(1)}, f32[256]{0:T(256)}, u32[]{:S(2)}) copy-start(f32[256]{0:T(256)} %get-tuple-element.612) | copy-start | bytes 3076
  879.0 52.5 %copy-start.112 = (f32[2048]{0:T(1024)S(1)}, f32[2048]{0:T(1024)}, u32[]{:S(2)}) copy-start(f32[2048]{0:T(1024)} %copy-done.111) | copy-start | bytes 24580
  (134 other events, 723.9 us)
Sparse Core Ops, SparseCore 0:
  653.3 130.8 reduce-scatter.6
  790.6 91.4 reduce-scatter.4
  885.0 134.0 reduce-scatter.8
  1021.7 130.8 reduce-scatter.10
where the time goes:
time: 1170 us; the launch traced here: 1160 us
  matrix products  405 us (35%)
  blocking collectives  244 us (21%)
  waiting for transfers between devices  209 us (18%)
  local copies, waits for them, and re-layouts  155 us (13%)
  other arithmetic  113 us (10%)
  loops' own time  17.9 us (2%)
  between operations  15.9 us (1%)
    reduce_scatter x2, waiting for transfers between devices, on_device(): lax.psum_scatter(feed_total, 'fsdp', scatter_dimension=0, tiled=True)  209 us
    unnamed x2, blocking collectives  79.4 us
    dot_general x8, matrix products, one_block(): jnp.einsum('shqk,skhd->sqhd', probs, values, preferred_element_type=jnp.f...  59.8 us
    unnamed x288, local copies, waits for them, and re-layouts  53.6 us
    dot_general x4, matrix products, one_block(): jnp.einsum('sqhd,skhd->shqk', g_block, values, preferred_element_type=jnp...  46.5 us
    dot_general x2, matrix products, forward_loop(): jnp.dot(active, reduce_w, preferred_element_type=jnp.float32)  45.9 us
    convert_element_type x4, other arithmetic, one_block(): d_scores = (probs * (d_probs - inner)).astype(jnp.bfloat16)  44.2 us
    all_gather x1, blocking collectives, on_device(): lax.all_gather(exit_weight, 'fsdp', axis=0, tiled=True)  43.4 us
  transfers between devices with their start and end apart: 4, of which 2 were waited for; matrix products, arithmetic and copies ran while one was open for 21% of the time, Pallas kernels for 0%

commit v1 on v0

v1 whole, which is shorter than its diff:
```python
import functools
import math
import jax
import jax.numpy as jnp
from jax import lax
from jax.experimental import pallas as pl
from jax.experimental.pallas import tpu as pltpu
from jax.sharding import PartitionSpec as P

F32, BF16 = jnp.float32, jnp.bfloat16
LEN = 1024
LOOPS = 2
EPS = 1e-05
D = 256
FF = 1024
HD = 64
LOG2E = 1.4426950408889634
LN2 = 0.6931471805599453
BLK = 256
NEG = -1e30


def dot_nn(a, b):
    return lax.dot_general(a, b, (((1,), (0,)), ((), ())), preferred_element_type=F32)


def dot_nt(a, b):
    return lax.dot_general(a, b, (((1,), (1,)), ((), ())), preferred_element_type=F32)


def dot_tn(a, b):
    return lax.dot_general(a, b, (((0,), (0,)), ((), ())), preferred_element_type=F32)


def norm_parts(x):
    mean = jnp.mean(x, axis=-1, keepdims=True)
    center = x - mean
    var = jnp.mean(center * center, axis=-1, keepdims=True)
    rstd = lax.rsqrt(var + EPS)
    return center * rstd, rstd


def norm_pull(xhat, rstd, gain, dy):
    dn = dy * gain
    m1 = jnp.mean(dn, axis=-1, keepdims=True)
    m2 = jnp.mean(dn * xhat, axis=-1, keepdims=True)
    return rstd * (dn - m1 - xhat * m2)


def gelu_parts(x):
    z = jnp.abs(x)
    t = 1.0 / (1.0 + (0.3275911 / math.sqrt(2.0)) * z)
    e = jnp.exp2((-0.5 * LOG2E) * (x * x))
    poly = t * (0.5 * 0.254829592 + t * (0.5 * -0.284496736 + t * (0.5 * 1.421413741 + t * (0.5 * -1.453152027 + t * (0.5 * 1.061405429)))))
    tail = poly * e
    cdf = jnp.where(x >= 0.0, 1.0 - tail, tail)
    return cdf, e


INV_SQRT_2PI = 1.0 / math.sqrt(2.0 * math.pi)


def lane_iota(rows):
    return lax.broadcasted_iota(jnp.int32, (rows, 128), 1)


def three_parts(x):
    hi = x.astype(BF16).astype(F32)
    r = x - hi
    mid = r.astype(BF16).astype(F32)
    return hi, mid, r - mid


def spread_parts(x, lane, spare):
    hi, mid, lo = three_parts(x)
    return jnp.where(lane == spare, hi, jnp.where(lane == spare + 1, mid, jnp.where(lane == spare + 2, lo, 0.0)))


def attn_forward(qkv, p, att, lx, vx, seqs):
    nblk = LEN // BLK

    def body(it, carry):
        s = it // 2
        pair = it % 2
        r0 = pl.multiple_of(s * LEN, LEN)
        cq = pl.multiple_of(pair * 128, 128)
        ck = pl.multiple_of(D + pair * 128, 128)
        cv = pl.multiple_of(2 * D + pair * 128, 128)
        lane = lane_iota(LEN)
        v = qkv[p, pl.ds(r0, LEN), pl.ds(cv, 128)]
        one = jnp.ones((LEN, 128), BF16)
        vx[0] = jnp.where(lane < HD, v, one)
        vx[1] = jnp.where(lane < HD, one, v)
        laneb = lane_iota(BLK)
        keep = lax.broadcasted_iota(jnp.int32, (BLK, BLK), 1) <= lax.broadcasted_iota(jnp.int32, (BLK, BLK), 0)
        for j in range(nblk):
            rows = pl.ds(pl.multiple_of(r0 + j * BLK, BLK), BLK)
            q = qkv[p, rows, pl.ds(cq, 128)]
            zero = jnp.zeros_like(q)
            outs, pieces = [], []
            for h in range(2):
                mine = (laneb < HD) if h == 0 else (laneb >= HD)
                qm = jnp.where(mine, q, zero)
                m_rows = (j + 1) * BLK
                k = qkv[p, pl.ds(r0, m_rows), pl.ds(ck, 128)]
                sc = dot_nt(qm, k)
                diag = jnp.where(keep, sc[:, j * BLK:], NEG)
                sc = jnp.concatenate([sc[:, : j * BLK], diag], axis=1) if j else diag
                top = jnp.max(sc, axis=-1, keepdims=True)
                pr = jnp.exp2(sc - top).astype(BF16)
                ox = dot_nn(pr, vx[h, :m_rows])
                den = pltpu.roll(ox, HD, 1)
                outs.append(ox / den)
                lse = top + jnp.log(ox) * LOG2E
                lse = jnp.where(mine, 0.0, lse)
                pieces.append(spread_parts(-lse, laneb, HD if h == 0 else 0))
            att[p, rows, pl.ds(cq, 128)] = jnp.where(laneb < HD, outs[0], outs[1]).astype(BF16)
            lx[p, rows, pl.ds(cq, 128)] = jnp.where(laneb < HD, pieces[1], pieces[0]).astype(BF16)
        return carry

    lax.fori_loop(0, seqs * 2, body, 0)


def attn_backward(qkv, p, att, lx, dmid_att, vx, kx, qx, dox, dk, dv, dq, seqs):
    nblk = LEN // BLK

    def body(it, carry):
        s = it // 2
        pair = it % 2
        r0 = pl.multiple_of(s * LEN, LEN)
        cq = pl.multiple_of(pair * 128, 128)
        ck = pl.multiple_of(D + pair * 128, 128)
        cv = pl.multiple_of(2 * D + pair * 128, 128)
        lane = lane_iota(LEN)
        seq = pl.ds(r0, LEN)
        low = lane < HD
        one = jnp.ones((LEN, 128), BF16)
        v = qkv[p, seq, pl.ds(cv, 128)]
        vx[0] = jnp.where(low, v, one)
        vx[1] = jnp.where(low, one, v)
        k = qkv[p, seq, pl.ds(ck, 128)]
        kx[0] = jnp.where(low, k, one)
        kx[1] = jnp.where(low, one, k)
        q = qkv[p, seq, pl.ds(cq, 128)]
        ls = lx[p, seq, pl.ds(cq, 128)]
        qx[0] = jnp.where(low, q, ls)
        qx[1] = jnp.where(low, ls, q)
        do = dmid_att[seq, pl.ds(cq, 128)]
        dof = do.astype(F32)
        prod = dof * att[p, seq, pl.ds(cq, 128)].astype(F32)
        in0 = jnp.sum(jnp.where(low, prod, 0.0), axis=-1, keepdims=True)
        in1 = jnp.sum(jnp.where(low, 0.0, prod), axis=-1, keepdims=True)
        dox[0] = jnp.where(low, dof, spread_parts(jnp.broadcast_to(-in0, (LEN, 128)), lane, HD)).astype(BF16)
        dox[1] = jnp.where(low, spread_parts(jnp.broadcast_to(-in1, (LEN, 128)), lane, 0), dof).astype(BF16)
        keep = lax.broadcasted_iota(jnp.int32, (BLK, BLK), 0) <= lax.broadcasted_iota(jnp.int32, (BLK, BLK), 1)
        for h in range(2):
            for j in reversed(range(nblk)):
                m = (j + 1) * BLK
                qj = qx[h, j * BLK:m]
                dj = dox[h, j * BLK:m]
                kk = kx[h, :m]
                st = dot_nt(kk, qj)
                pt = jnp.exp2(st)
                diag = jnp.where(keep, pt[j * BLK:], 0.0)
                pt = jnp.concatenate([pt[: j * BLK], diag], axis=0) if j else diag
                dpt = dot_nt(vx[h, :m], dj)
                dst = (pt * dpt).astype(BF16)
                ptb = pt.astype(BF16)
                if j == nblk - 1:
                    dv[h, :m] = dot_nn(ptb, dj)
                    dk[h, :m] = dot_nn(dst, qj)
                else:
                    dv[h, :m] += dot_nn(ptb, dj)
                    dk[h, :m] += dot_nn(dst, qj)
                dq[h, j * BLK:m] = dot_tn(dst, kk)
        qkv[p, seq, pl.ds(cq, 128)] = (jnp.where(low, dq[0], dq[1]) * 0.125).astype(BF16)
        qkv[p, seq, pl.ds(ck, 128)] = (jnp.where(low, dk[0], dk[1]) * LN2).astype(BF16)
        qkv[p, seq, pl.ds(cv, 128)] = jnp.where(low, dv[0], dv[1]).astype(BF16)
        return carry

    lax.fori_loop(0, seqs * 2, body, 0)


def compute_kernel(
    state_in, embed_in, grad_in, entry_w, exit_w, expand_w, reduce_w, lead_g, lead_s, mid_g, mid_s, exp_b, red_b,
    final_out, grad, embed_total, g_entry, g_exit, g_expand, g_reduce, g_small,
    mixed, qkv, att, lx, middle, active, gelup, datt, entry_t, exit_t, expand_t, reduce_t,
    vx, kx, qx, dox, dk, dv, dq, g_reduce_t, g_exp_b, *, tokens,
):
    seqs = tokens // LEN
    RA, RF, RC = 512, 512, 512

    def tiles(rows, fn):
        def body(i, c):
            fn(pl.ds(pl.multiple_of(i * rows, rows), rows))
            return c
        lax.fori_loop(0, tokens // rows, body, 0)

    lg, ls_, mg, ms = (r[...].astype(F32) for r in (lead_g, lead_s, mid_g, mid_s))
    eb, rb = exp_b[...].astype(F32), red_b[...].astype(F32)
    entry_t[...] = entry_w[...].T
    exit_t[...] = exit_w[...].T
    expand_t[...] = expand_w[...].T
    reduce_t[...] = reduce_w[...].T
    g_entry[...] = jnp.zeros_like(g_entry)
    g_exit[...] = jnp.zeros_like(g_exit)
    g_expand[...] = jnp.zeros_like(g_expand)
    g_reduce_t[...] = jnp.zeros_like(g_reduce_t)
    g_small[...] = jnp.zeros_like(g_small)
    g_exp_b[...] = jnp.zeros_like(g_exp_b)

    def enter(p):
        def fn(rows):
            e = embed_in[rows, :].astype(F32)
            x = (state_in[rows, :].astype(F32) if p == 0 else grad[rows, :]) + e
            mixed[p, rows, :] = x
            xhat, _ = norm_parts(x)
            n = (xhat * lg + ls_).astype(BF16)
            y = dot_nn(n, entry_w[...])
            qkv[p, rows, :D] = (y[:, :D] * (LOG2E * 0.125)).astype(BF16)
            qkv[p, rows, D:] = y[:, D:].astype(BF16)
        tiles(RA, fn)

    def feed_forward(p, rows):
        mid = mixed[p, rows, :] + dot_nn(att[p, rows, :], exit_w[...])
        middle[p, rows, :] = mid
        xhat, rstd = norm_parts(mid)
        n2 = (xhat * mg + ms).astype(BF16)
        hid = dot_nn(n2, expand_w[...]) + eb
        cdf, e = gelu_parts(hid)
        act = (hid * cdf).astype(BF16)
        gp = cdf + hid * (e * INV_SQRT_2PI)
        res = mid + dot_nn(act, reduce_w[...]) + rb
        return mid, xhat, rstd, n2, act, gp, res

    def feed_backward(p, rows, g, xhat, rstd, n2, act, gp):
        d_out = g.astype(BF16)
        g_small[5:6, :] += jnp.sum(g, axis=0, keepdims=True)
        g_reduce_t[...] += dot_tn(d_out, act)
        dh = dot_nn(d_out, reduce_t[...]) * gp
        g_exp_b[...] += jnp.sum(dh, axis=0, keepdims=True)
        dh = dh.astype(BF16)
        g_expand[...] += dot_tn(n2, dh)
        dn = dot_nn(dh, expand_t[...])
        g_small[2:3, :] += jnp.sum(dn * xhat, axis=0, keepdims=True)
        g_small[3:4, :] += jnp.sum(dn, axis=0, keepdims=True)
        dm = g + norm_pull(xhat, rstd, mg, dn)
        grad[rows, :] = dm
        db = dm.astype(BF16)
        g_exit[...] += dot_tn(att[p, rows, :], db)
        datt[rows, :] = dot_nn(db, exit_t[...]).astype(BF16)

    def ff_first(rows):
        mid, xhat, rstd, n2, act, gp, res = feed_forward(0, rows)
        active[rows, :] = act
        gelup[rows, :] = gp.astype(BF16)
        grad[rows, :] = res

    def ff_last(rows):
        mid, xhat, rstd, n2, act, gp, res = feed_forward(1, rows)
        final_out[rows, :] = res.astype(BF16)
        feed_backward(1, rows, grad_in[rows, :].astype(F32), xhat, rstd, n2, act, gp)

    def ff_back(rows):
        xhat, rstd = norm_parts(middle[0, rows, :])
        n2 = (xhat * mg + ms).astype(BF16)
        feed_backward(0, rows, grad[rows, :], xhat, rstd, n2, active[rows, :], gelup[rows, :].astype(F32))

    def leave(p):
        def fn(rows):
            xhat, rstd = norm_parts(mixed[p, rows, :])
            n = (xhat * lg + ls_).astype(BF16)
            dqkv = qkv[p, rows, :]
            g_entry[...] += dot_tn(n, dqkv)
            dn = dot_nn(dqkv, entry_t[...])
            g_small[0:1, :] += jnp.sum(dn * xhat, axis=0, keepdims=True)
            g_small[1:2, :] += jnp.sum(dn, axis=0, keepdims=True)
            g = grad[rows, :] + norm_pull(xhat, rstd, lg, dn)
            grad[rows, :] = g
            embed_total[rows, :] = g if p == 1 else embed_total[rows, :] + g
        tiles(RC, fn)

    enter(0)
    attn_forward(qkv, 0, att, lx, vx, seqs)
    tiles(RF, ff_first)
    enter(1)
    attn_forward(qkv, 1, att, lx, vx, seqs)
    tiles(RF, ff_last)
    attn_backward(qkv, 1, att, lx, datt, vx, kx, qx, dox, dk, dv, dq, seqs)
    leave(1)
    tiles(RF, ff_back)
    attn_backward(qkv, 0, att, lx, datt, vx, kx, qx, dox, dk, dv, dq, seqs)
    leave(0)
    g_reduce[...] = g_reduce_t[...].T
    for i in range(4):
        g_small[8 + i:9 + i, :] = g_exp_b[:, i * D:(i + 1) * D]


def compute(tokens):
    T = tokens
    sds = jax.ShapeDtypeStruct
    vm = pl.BlockSpec(memory_space=pltpu.VMEM)
    return pl.pallas_call(
        functools.partial(compute_kernel, tokens=tokens),
        in_specs=[vm] * 13,
        out_specs=[vm] * 8,
        out_shape=[
            sds((T, D), BF16), sds((T, D), F32), sds((T, D), F32),
            sds((D, 3 * D), F32), sds((D, D), F32), sds((D, FF), F32), sds((FF, D), F32), sds((16, D), F32),
        ],
        scratch_shapes=[
            pltpu.VMEM((2, T, D), F32), pltpu.VMEM((2, T, 3 * D), BF16), pltpu.VMEM((2, T, D), BF16), pltpu.VMEM((2, T, D), BF16),
            pltpu.VMEM((2, T, D), F32), pltpu.VMEM((T, FF), BF16), pltpu.VMEM((T, FF), BF16), pltpu.VMEM((T, D), BF16),
            pltpu.VMEM((3 * D, D), BF16), pltpu.VMEM((D, D), BF16), pltpu.VMEM((FF, D), BF16), pltpu.VMEM((D, FF), BF16),
            pltpu.VMEM((2, LEN, 128), BF16), pltpu.VMEM((2, LEN, 128), BF16), pltpu.VMEM((2, LEN, 128), BF16), pltpu.VMEM((2, LEN, 128), BF16),
            pltpu.VMEM((2, LEN, 128), F32), pltpu.VMEM((2, LEN, 128), F32), pltpu.VMEM((2, LEN, 128), F32),
            pltpu.VMEM((D, FF), F32), pltpu.VMEM((1, FF), F32),
        ],
        compiler_params=pltpu.CompilerParams(vmem_limit_bytes=62 * 1024 * 1024),
        name="compute",
    )


def on_device(loop_state, embedding, output_grad, entry_weight, exit_weight, lead_gain, lead_shift, expand_weight, reduce_weight, middle_gain, middle_shift, expand_bias, reduce_bias):
    n = lax.axis_size("fsdp")
    tokens = loop_state.shape[0]
    shards = (entry_weight, exit_weight, expand_weight, reduce_weight, lead_gain, lead_shift, middle_gain, middle_shift, expand_bias, reduce_bias)
    packed = jnp.concatenate([a.reshape(-1) for a in shards])
    whole = lax.all_gather(packed, "fsdp", axis=0)
    full, at = [], 0
    for a in shards:
        full.append(whole[:, at : at + a.size].reshape((n * a.shape[0],) + a.shape[1:]))
        at += a.size
    entry_w, exit_w, expand_w, reduce_w, lg, ls, mg, ms, eb, rb = full
    row = lambda a: a.reshape(1, -1)
    final, grad, total, g_entry, g_exit, g_expand, g_reduce, small = compute(tokens)(
        loop_state, embedding, output_grad, entry_w, exit_w, expand_w, reduce_w, row(lg), row(ls), row(mg), row(ms), row(eb), row(rb)
    )
    terms = (g_entry, g_exit, g_expand, g_reduce, small[0], small[1], small[2], small[3], small[8:12].reshape(-1), small[5])
    sums = lax.psum_scatter(jnp.concatenate([a.reshape(n, -1) for a in terms], axis=1), "fsdp", scatter_dimension=0, tiled=True)[0]
    outs, at = [], 0
    for a in terms:
        shape = (a.shape[0] // n,) + a.shape[1:]
        size = a.size // n
        outs.append(sums[at : at + size].reshape(shape))
        at += size
    entry_g, exit_g, expand_g, reduce_g, lgg, lsg, mgg, msg, ebg, rbg = outs
    return (final, grad, total, entry_g, exit_g, lgg, lsg, expand_g, reduce_g, mgg, msg, ebg, rbg)


def solution(mesh):
    two, one = P("fsdp", None), P("fsdp")
    in_specs = (two, two, two, two, two, one, one, two, two, one, one, one, one)
    out_specs = (two, two, two, two, two, one, one, two, two, one, one, one, one)
    return jax.shard_map(on_device, mesh=mesh, in_specs=in_specs, out_specs=out_specs, check_vma=False)
```

time: 1170 us -> 438 us (0.37)
  matrix products: 405 us -> 0 us
  blocking collectives: 244 us -> 0 us
  local copies, waits for them, and re-layouts: 155 us -> 37.3 us
  Pallas kernels: 0 us -> 113 us
  other arithmetic: 113 us -> 0 us
  waiting for transfers between devices: 209 us -> 272 us
  loops' own time: 17.9 us -> 0 us
    dot_general x58 -> x0, matrix products: 363 us -> none  [the longest x8 59.8 us: one_block(): jnp.einsum('shqk,skhd->sqhd', probs, values, preferred_element_type=jnp.f...]
    unnamed x4, waiting for transfers between devices: 0.07 us -> 272 us
    reduce_scatter x4 -> x0, waiting for transfers between devices: 209 us -> none  [the longest x2 209 us: on_device(): lax.psum_scatter(feed_total, 'fsdp', scatter_dimension=0, tiled=True)]
    all_gather x4 -> x0, blocking collectives: 165 us -> none  [the longest x1 43.4 us: on_device(): lax.all_gather(exit_weight, 'fsdp', axis=0, tiled=True)]
    pallas_call x0 -> x1, Pallas kernels: none -> 113 us  [on_device(): compute(tokens)]
    unnamed x2 -> x0, blocking collectives: 79.4 us -> none
    unnamed x288 -> x9, local copies, waits for them, and re-layouts: 53.6 us -> 4 us
    convert_element_type x12 -> x0, other arithmetic: 48.3 us -> none  [the longest x4 44.2 us: one_block(): d_scores = (probs * (d_probs - inner)).astype(jnp.bfloat16)]
  transfers between devices with their start and end apart: 4 -> 2, of which waited for: 2 -> 2; matrix products, arithmetic and copies ran while one was open for 21% -> 0% of each run, Pallas kernels for 0% -> 0%
where the time goes in v1:
time: 438 us; the launch traced here: 437 us
  waiting for transfers between devices  272 us (62%)
  Pallas kernels  113 us (26%)
  local copies, waits for them, and re-layouts  37.3 us (9%)
  between operations  14.2 us (3%)
    unnamed x4, waiting for transfers between devices  272 us
    pallas_call x1, Pallas kernels, on_device(): compute(tokens)  113 us
  transfers between devices with their start and end apart: 2, of which 2 were waited for; matrix products, arithmetic and copies ran while one was open for 0% of the time, Pallas kernels for 0%

profile of v1, /device:TPU:0, one launch (start us, length us, event | category | flops | bytes accessed | tf_op | source)
XLA Modules:
  0.0 437.2 jit_solution(15755671340481247251)
XLA Ops:
  7.2 0.7 reshape.88
  8.0 0.7 copy.26
  8.7 0.7 copy.30
  9.4 0.7 copy.28
  10.1 4.1 concatenate.6
  15.0 1.1 copy-done
  16.2 134.3 %all-reduce.5.cloned.1.call-done = bf16[788736]{0:T(1024)(128)(2,1)} async-done(((bf16[788736]{0:T(1024)(128)(2,1)}), bf16[788736]{0:T(1024)(128)(2,1)}) %all-reduce.5.cloned.1.call-update) | async-done | bytes 1577488
  150.5 3.7 reshape.104
  154.4 0.9 reshape.92.entry_w
  155.3 0.7 reshape.93.exit_w
  156.1 1.1 reshape.94.expand_w
  157.1 1.0 reshape.95.reduce_w
  158.2 0.7 reshape_reshape.21.lead_g
  158.8 0.7 reshape_reshape.22.lead_s
  159.5 0.7 reshape_reshape.23.mid_g
  160.1 0.7 reshape_reshape.24.mid_s
  160.8 0.7 reshape_reshape.25.exp_b
  161.5 0.7 reshape_reshape.26.red_b
  162.2 113.3 %compute.1 = (bf16[2048,256]{1,0:T(8,128)(2,1)}, f32[2048,256]{1,0:T(8,128)}, f32[2048,256]{1,0:T(8,128)}, f32[256,768]{1,0:T(8,128)}, f32[256,256]{1,0:T(8,128)...) custom-call(bf16[2048,256]{1,0:T(8,128)(2,1)} %state_in.1, bf16[2048,256]{1,0:T(8,128)(2,1)} %embed_in.1, ...), custom_call_target="tpu_custom_call" | custom-call | tf_op jit(solution)/shard_map/compute/pallas_call | solution.py:336
  275.5 0.9 slice_reduce_fusion
  276.4 0.7 slice.114
  277.1 1.3 reshape.96
  278.4 1.0 reshape.97
  279.6 1.4 reshape.99
  281.5 2.4 concatenate.7
  283.9 138.1 %all-reduce.7.cloned.1.call-done = f32[32,24648]{1,0:T(8,128)} async-done(((f32[32,24648]{1,0:T(8,128)}), f32[32,24648]{1,0:T(8,128)}) %all-reduce.7.cloned.1.call-update) | async-done | bytes 3154960
  422.0 1.0 dynamic-slice_reduce_fusion.2
  423.6 1.0 dynamic-slice_reduce_fusion.3
  425.2 1.3 dynamic-slice_reduce_fusion
  426.4 0.6 reshape.102
  427.7 1.3 dynamic-slice_bitcast_fusion.1
  428.9 1.5 dynamic-slice_bitcast_fusion
  (24 shorter events, 3.6 us)
Async XLA Ops:
  7.2 143.3 %all-reduce.5.cloned.1.call-start = ((), (), s32[]{:S(2)}) async-start(), calls=%async_computation | async-start | bytes 3158016
  15.0 1.1 copy-start
  16.1 405.8 %all-reduce.7.cloned.1.call-start = ((), (), s32[]{:S(2)}) async-start(), calls=%async_computation.1 | async-start | bytes 6324224
  275.5 3.9 copy-start.1
Sparse Core Ops, SparseCore 0:
  16.3 134.1 all-reduce.4
  284.0 137.8 all-reduce.6

commit v2 on v1

v2 whole, which is shorter than its diff:
```python
import functools
import math
import jax
import jax.numpy as jnp
from jax import lax
from jax.experimental import pallas as pl
from jax.experimental.pallas import tpu as pltpu
from jax.sharding import PartitionSpec as P
from types import SimpleNamespace

F32, BF16 = jnp.float32, jnp.bfloat16
LEN = 1024
LOOPS = 2
EPS = 1e-05
D = 256
FF = 1024
HD = 64
LOG2E = 1.4426950408889634
LN2 = 0.6931471805599453
BLK = 256
NEG = -1e30


def dot_nn(a, b):
    return lax.dot_general(a, b, (((1,), (0,)), ((), ())), preferred_element_type=F32)


def dot_nt(a, b):
    return lax.dot_general(a, b, (((1,), (1,)), ((), ())), preferred_element_type=F32)


def dot_tn(a, b):
    return lax.dot_general(a, b, (((0,), (0,)), ((), ())), preferred_element_type=F32)


def norm_parts(x):
    mean = jnp.mean(x, axis=-1, keepdims=True)
    center = x - mean
    var = jnp.mean(center * center, axis=-1, keepdims=True)
    rstd = lax.rsqrt(var + EPS)
    return center * rstd, rstd


def norm_pull(xhat, rstd, gain, dy):
    dn = dy * gain
    m1 = jnp.mean(dn, axis=-1, keepdims=True)
    m2 = jnp.mean(dn * xhat, axis=-1, keepdims=True)
    return rstd * (dn - m1 - xhat * m2)


def gelu_parts(x):
    z = jnp.abs(x)
    t = 1.0 / (1.0 + (0.3275911 / math.sqrt(2.0)) * z)
    e = jnp.exp2((-0.5 * LOG2E) * (x * x))
    poly = t * (0.5 * 0.254829592 + t * (0.5 * -0.284496736 + t * (0.5 * 1.421413741 + t * (0.5 * -1.453152027 + t * (0.5 * 1.061405429)))))
    tail = poly * e
    cdf = jnp.where(x >= 0.0, 1.0 - tail, tail)
    return cdf, e


INV_SQRT_2PI = 1.0 / math.sqrt(2.0 * math.pi)


def lane_iota(rows):
    return lax.broadcasted_iota(jnp.int32, (rows, 128), 1)


def three_parts(x):
    hi = x.astype(BF16).astype(F32)
    r = x - hi
    mid = r.astype(BF16).astype(F32)
    return hi, mid, r - mid


def spread_parts(x, lane, spare):
    hi, mid, lo = three_parts(x)
    return jnp.where(lane == spare, hi, jnp.where(lane == spare + 1, mid, jnp.where(lane == spare + 2, lo, 0.0)))


def attn_forward(qkv, p, att, lx, vx, seqs, hook=None):
    nblk = LEN // BLK

    def body(it, carry):
        if hook is not None:
            hook(it)
        s = it // 2
        pair = it % 2
        r0 = pl.multiple_of(s * LEN, LEN)
        cq = pl.multiple_of(pair * 128, 128)
        ck = pl.multiple_of(D + pair * 128, 128)
        cv = pl.multiple_of(2 * D + pair * 128, 128)
        lane = lane_iota(LEN)
        v = qkv[p, pl.ds(r0, LEN), pl.ds(cv, 128)]
        one = jnp.ones((LEN, 128), BF16)
        vx[0] = jnp.where(lane < HD, v, one)
        vx[1] = jnp.where(lane < HD, one, v)
        laneb = lane_iota(BLK)
        keep = lax.broadcasted_iota(jnp.int32, (BLK, BLK), 1) <= lax.broadcasted_iota(jnp.int32, (BLK, BLK), 0)
        for j in range(nblk):
            rows = pl.ds(pl.multiple_of(r0 + j * BLK, BLK), BLK)
            q = qkv[p, rows, pl.ds(cq, 128)]
            zero = jnp.zeros_like(q)
            outs, pieces = [], []
            for h in range(2):
                mine = (laneb < HD) if h == 0 else (laneb >= HD)
                qm = jnp.where(mine, q, zero)
                m_rows = (j + 1) * BLK
                k = qkv[p, pl.ds(r0, m_rows), pl.ds(ck, 128)]
                sc = dot_nt(qm, k)
                diag = jnp.where(keep, sc[:, j * BLK:], NEG)
                sc = jnp.concatenate([sc[:, : j * BLK], diag], axis=1) if j else diag
                top = jnp.max(sc, axis=-1, keepdims=True)
                pr = jnp.exp2(sc - top).astype(BF16)
                ox = dot_nn(pr, vx[h, :m_rows])
                den = pltpu.roll(ox, HD, 1)
                outs.append(ox / den)
                lse = top + jnp.log(ox) * LOG2E
                lse = jnp.where(mine, 0.0, lse)
                pieces.append(spread_parts(-lse, laneb, HD if h == 0 else 0))
            att[p, rows, pl.ds(cq, 128)] = jnp.where(laneb < HD, outs[0], outs[1]).astype(BF16)
            lx[p, rows, pl.ds(cq, 128)] = jnp.where(laneb < HD, pieces[1], pieces[0]).astype(BF16)
        return carry

    lax.fori_loop(0, seqs * 2, body, 0)


def attn_backward(qkv, p, att, lx, dmid_att, vx, kx, qx, dox, dk, dv, dq, seqs, hook=None):
    nblk = LEN // BLK

    def body(it, carry):
        if hook is not None:
            hook(it)
        s = it // 2
        pair = it % 2
        r0 = pl.multiple_of(s * LEN, LEN)
        cq = pl.multiple_of(pair * 128, 128)
        ck = pl.multiple_of(D + pair * 128, 128)
        cv = pl.multiple_of(2 * D + pair * 128, 128)
        lane = lane_iota(LEN)
        seq = pl.ds(r0, LEN)
        low = lane < HD
        one = jnp.ones((LEN, 128), BF16)
        v = qkv[p, seq, pl.ds(cv, 128)]
        vx[0] = jnp.where(low, v, one)
        vx[1] = jnp.where(low, one, v)
        k = qkv[p, seq, pl.ds(ck, 128)]
        kx[0] = jnp.where(low, k, one)
        kx[1] = jnp.where(low, one, k)
        q = qkv[p, seq, pl.ds(cq, 128)]
        ls = lx[p, seq, pl.ds(cq, 128)]
        qx[0] = jnp.where(low, q, ls)
        qx[1] = jnp.where(low, ls, q)
        do = dmid_att[seq, pl.ds(cq, 128)]
        dof = do.astype(F32)
        prod = dof * att[p, seq, pl.ds(cq, 128)].astype(F32)
        in0 = jnp.sum(jnp.where(low, prod, 0.0), axis=-1, keepdims=True)
        in1 = jnp.sum(jnp.where(low, 0.0, prod), axis=-1, keepdims=True)
        dox[0] = jnp.where(low, dof, spread_parts(jnp.broadcast_to(-in0, (LEN, 128)), lane, HD)).astype(BF16)
        dox[1] = jnp.where(low, spread_parts(jnp.broadcast_to(-in1, (LEN, 128)), lane, 0), dof).astype(BF16)
        keep = lax.broadcasted_iota(jnp.int32, (BLK, BLK), 0) <= lax.broadcasted_iota(jnp.int32, (BLK, BLK), 1)
        for h in range(2):
            for j in reversed(range(nblk)):
                m = (j + 1) * BLK
                qj = qx[h, j * BLK:m]
                dj = dox[h, j * BLK:m]
                kk = kx[h, :m]
                st = dot_nt(kk, qj)
                pt = jnp.exp2(st)
                diag = jnp.where(keep, pt[j * BLK:], 0.0)
                pt = jnp.concatenate([pt[: j * BLK], diag], axis=0) if j else diag
                dpt = dot_nt(vx[h, :m], dj)
                dst = (pt * dpt).astype(BF16)
                ptb = pt.astype(BF16)
                if j == nblk - 1:
                    dv[h, :m] = dot_nn(ptb, dj)
                    dk[h, :m] = dot_nn(dst, qj)
                else:
                    dv[h, :m] += dot_nn(ptb, dj)
                    dk[h, :m] += dot_nn(dst, qj)
                dq[h, j * BLK:m] = dot_tn(dst, kk)
        qkv[p, seq, pl.ds(cq, 128)] = (jnp.where(low, dq[0], dq[1]) * 0.125).astype(BF16)
        qkv[p, seq, pl.ds(ck, 128)] = (jnp.where(low, dk[0], dk[1]) * LN2).astype(BF16)
        qkv[p, seq, pl.ds(cv, 128)] = jnp.where(low, dv[0], dv[1]).astype(BF16)
        return carry

    lax.fori_loop(0, seqs * 2, body, 0)


def digit_groups(n):
    groups = [(1, 2)]
    stride = 2
    while stride < n:
        size = min(4, n // stride)
        groups.append((stride, size))
        stride *= size
    return groups[::-1]


class Links:
    def __init__(self, n):
        self.groups = digit_groups(n)
        self.me = lax.axis_index("fsdp")
        self.digits = [(self.me // stride) % size for stride, size in self.groups]
        self.sizes = tuple(size for _, size in self.groups)

    def digit(self, g, t):
        return (self.digits[g] + t) % self.sizes[g]

    def peer(self, g, t):
        return self.me + (self.digit(g, t) - self.digits[g]) * self.groups[g][0]

    def barrier(self):
        sem = pltpu.get_barrier_semaphore()
        count = 0
        for g, size in enumerate(self.sizes):
            for t in range(1, size):
                pl.semaphore_signal(sem, inc=1, device_id=(self.peer(g, t),), device_id_type=pl.DeviceIdType.MESH)
                count += 1
        return lambda: pl.semaphore_wait(sem, count)

    def copy(self, src, dst, sems, g, t):
        return pltpu.make_async_remote_copy(
            src_ref=src,
            dst_ref=dst,
            send_sem=sems.at[0, g, t - 1],
            recv_sem=sems.at[1, g, t - 1],
            device_id=(self.peer(g, t),),
            device_id_type=pl.DeviceIdType.MESH,
        )

    def held(self, buf, g, t=0):
        tail = [self.digit(g, t)] + self.digits[g + 1:]
        return buf.at[(slice(None),) * g + tuple(tail)]

    def gather_start(self, buf, sems, g):
        for t in range(1, self.sizes[g]):
            self.copy(self.held(buf, g), self.held(buf, g), sems, g, t).start()

    def gather_wait(self, buf, sems, g):
        for t in range(1, self.sizes[g]):
            self.copy(self.held(buf, g), self.held(buf, g, -t), sems, g, t).wait_recv()
        for t in range(1, self.sizes[g]):
            self.copy(self.held(buf, g), self.held(buf, g), sems, g, t).wait_send()

    def reduce_start(self, part, got, sems, g):
        for t in range(1, self.sizes[g]):
            src = part.at[(slice(None),) * g + (self.digit(g, t),)]
            self.copy(src, got.at[t - 1], sems, g, t).start()

    def reduce_wait(self, part, got, sems, g):
        for t in range(1, self.sizes[g]):
            src = part.at[(slice(None),) * g + (self.digit(g, t),)]
            self.copy(src, got.at[t - 1], sems, g, t).wait()
        total = part[(slice(None),) * g + (self.digits[g],)].astype(F32)
        for t in range(1, self.sizes[g]):
            total = total + got[t - 1].astype(F32)
        return total


def pair_rows(x, t):
    return jnp.concatenate([x[:, 256 * t : 256 * t + 128], x[:, 256 * t + 128 : 256 * t + 256]], axis=0)


ENTRY_ROWS = 64
FEED_ROWS = 160


def mega_kernel(*refs, names, n, tokens, comm):
    o = SimpleNamespace(**dict(zip(names, refs)))
    seqs = tokens // LEN
    RA = RF = RC = 512

    def tiles(rows, fn):
        def body(i, c):
            fn(pl.ds(pl.multiple_of(i * rows, rows), rows))
            return c
        lax.fori_loop(0, tokens // rows, body, 0)

    def zero(*rs):
        for r in rs:
            r[...] = jnp.zeros_like(r)

    def pack_parameters():
        d = tuple(links.digits)
        x = o.entry_s[...].astype(F32)
        for t in range(3):
            o.buf1[d + (pl.ds(16 * t, 16),)] = pair_rows(x, t).astype(BF16)
        o.vec[...] = jnp.zeros_like(o.vec)
        for i, r in enumerate((o.lead_g, o.lead_s, o.mid_g, o.mid_s, o.red_b)):
            o.vec[i:i + 1, 0:8] = r[...].astype(F32).reshape(1, 8)
        o.vec[8:9, 0:32] = o.exp_b[...].astype(F32).reshape(1, 32)
        low = pltpu.roll(o.vec[0:8, :], (links.me * 8) % 128, 1)
        high = pltpu.roll(jnp.broadcast_to(o.vec[8:9, :], (8, 128)), (links.me * 32) % 128, 1)
        row = lax.broadcasted_iota(jnp.int32, (8, 128), 0)
        high = jnp.where(row == links.me // 4, high, 0.0)
        o.buf1[d + (pl.ds(48, 16),)] = jnp.concatenate([low, high], axis=0).astype(BF16)
        o.buf2[d + (pl.ds(0, 16),)] = pair_rows(o.exit_s[...].astype(F32), 0).astype(BF16)
        x = o.expand_s[...].astype(F32)
        for t in range(4):
            o.buf2[d + (pl.ds(16 + 16 * t, 16),)] = pair_rows(x, t).astype(BF16)
        for c in range(2):
            o.buf2[d + (pl.ds(80 + 32 * c, 32),)] = o.reduce_s[:, 128 * c:128 * c + 128]

    def unpack(buf, at, chunks, dst):
        for t in range(chunks // 2):
            x = buf[:, :, :, at + 16 * t:at + 16 * t + 16, :].astype(F32).reshape(n, 16, 128)
            dst[:, 256 * t:256 * t + 128] = x[:, :8].reshape(8 * n, 128).astype(BF16)
            dst[:, 256 * t + 128:256 * t + 256] = x[:, 8:].reshape(8 * n, 128).astype(BF16)

    def unpack_first():
        unpack(o.buf1, 0, 6, o.entry_w)
        v = o.buf1[:, :, :, 48:64, :].astype(F32).reshape(n, 16, 128)
        first = jnp.sum(v[: n // 2], axis=0)
        second = jnp.sum(v[n // 2:], axis=0)
        o.vecs[0:5, 0:128] = first[0:5]
        o.vecs[0:5, 128:256] = second[0:5]
        both = (first + second)[8:16]
        for c in range(8):
            o.eb[0:1, 128 * c:128 * c + 128] = both[c:c + 1]
        o.entry_t[...] = o.entry_w[...].T

    def unpack_second():
        unpack(o.buf2, 0, 2, o.exit_w)
        unpack(o.buf2, 16, 8, o.expand_w)
        for c in range(2):
            x = o.buf2[:, :, :, 80 + 32 * c:112 + 32 * c, :]
            o.reduce_w[:, 128 * c:128 * c + 128] = x.reshape(32 * n, 128)
        turn_second()

    def turn_second():
        o.exit_t[...] = o.exit_w[...].T
        o.expand_t[...] = o.expand_w[...].T
        o.reduce_t[...] = o.reduce_w[...].T

    def pack_gradient(part, at, chunks, grad):
        for t in range(chunks // 2):
            a = grad[:, 256 * t:256 * t + 128].reshape(n, 8, 128)
            b = grad[:, 256 * t + 128:256 * t + 256].reshape(n, 8, 128)
            x = jnp.concatenate([a, b], axis=1).astype(BF16)
            part[:, :, :, at + 16 * t:at + 16 * t + 16, :] = x.reshape(links.sizes + (16, 128))

    def pack_vectors(part, at, rows):
        x = jnp.concatenate(rows + [jnp.zeros((16 - len(rows), 128), F32)], axis=0) if len(rows) < 16 else jnp.concatenate(rows, axis=0)
        part[:, :, :, at:at + 16, :] = jnp.broadcast_to(x.astype(BF16), links.sizes + (16, 128))

    def halves(row):
        return [row[:, :128], row[:, 128:]]

    def own_eight(total, at):
        both = jnp.where(links.me >= n // 2, total[at + 1:at + 2], total[at:at + 1])
        both = pltpu.roll(jnp.broadcast_to(both, (8, 128)), (128 - (links.me * 8) % 128) % 128, 1)
        return both[0:1, 0:8].reshape(8)

    def feed_reduce_pack():
        pack_gradient(o.buf2, 0, 2, o.g_exit)
        pack_gradient(o.buf2, 16, 8, o.g_expand)
        for c in range(2):
            x = o.g_reduce_t[128 * c:128 * c + 128, :].T.astype(BF16)
            o.buf2[:, :, :, 80 + 32 * c:112 + 32 * c, :] = x.reshape(links.sizes + (32, 128))
        rows = halves(o.g_small[2:3, :]) + halves(o.g_small[3:4, :]) + halves(o.g_small[5:6, :])
        rows += [o.g_exp_b[:, 128 * c:128 * c + 128] for c in range(8)]
        pack_vectors(o.buf2, 144, rows)

    def feed_reduce_end(total):
        for c in range(2):
            o.exit_o[:, 128 * c:128 * c + 128] = total[8 * c:8 * c + 8]
            o.reduce_o[:, 128 * c:128 * c + 128] = total[80 + 32 * c:112 + 32 * c]
        for c in range(8):
            o.expand_o[:, 128 * c:128 * c + 128] = total[16 + 8 * c:24 + 8 * c]
        o.mid_g_o[...] = own_eight(total, 144)
        o.mid_s_o[...] = own_eight(total, 146)
        o.red_b_o[...] = own_eight(total, 148)
        row = lax.broadcasted_iota(jnp.int32, (8, 128), 0)
        x = jnp.sum(jnp.where(row == links.me // 4, total[150:158], 0.0), axis=0, keepdims=True)
        x = pltpu.roll(jnp.broadcast_to(x, (8, 128)), (128 - (links.me * 32) % 128) % 128, 1)
        o.exp_b_o[...] = x[0:1, 0:32].reshape(32)

    def entry_reduce_pack():
        pack_gradient(o.buf1, 0, 6, o.g_entry)
        pack_vectors(o.buf1, 48, halves(o.g_small[0:1, :]) + halves(o.g_small[1:2, :]))

    def entry_reduce_end(total):
        for c in range(6):
            o.entry_o[:, 128 * c:128 * c + 128] = total[8 * c:8 * c + 8]
        o.lead_g_o[...] = own_eight(total, 48)
        o.lead_s_o[...] = own_eight(total, 50)

    def enter(p):
        lg, ls = o.vecs[0:1, :], o.vecs[1:2, :]

        def fn(rows):
            e = o.embed_in[rows, :].astype(F32)
            x = (o.state_in[rows, :].astype(F32) if p == 0 else o.grad[rows, :]) + e
            o.mixed[p, rows, :] = x
            xhat, _ = norm_parts(x)
            y = dot_nn((xhat * lg + ls).astype(BF16), o.entry_w[...])
            o.qkv[p, rows, :D] = (y[:, :D] * (LOG2E * 0.125)).astype(BF16)
            o.qkv[p, rows, D:] = y[:, D:].astype(BF16)
        tiles(RA, fn)

    def feed_forward(p, rows):
        mg, ms, rb = o.vecs[2:3, :], o.vecs[3:4, :], o.vecs[4:5, :]
        mid = o.mixed[p, rows, :] + dot_nn(o.att[p, rows, :], o.exit_w[...])
        xhat, rstd = norm_parts(mid)
        n2 = (xhat * mg + ms).astype(BF16)
        hid = dot_nn(n2, o.expand_w[...]) + o.eb[...]
        cdf, e = gelu_parts(hid)
        act = (hid * cdf).astype(BF16)
        gp = cdf + hid * (e * INV_SQRT_2PI)
        res = mid + dot_nn(act, o.reduce_w[...]) + rb
        return mid, xhat, rstd, n2, act, gp, res

    def feed_backward(p, rows, g, xhat, rstd, n2, act, gp):
        d_out = g.astype(BF16)
        o.g_small[5:6, :] += jnp.sum(g, axis=0, keepdims=True)
        o.g_reduce_t[...] += dot_tn(d_out, act)
        dh = dot_nn(d_out, o.reduce_t[...]) * gp
        o.g_exp_b[...] += jnp.sum(dh, axis=0, keepdims=True)
        dh = dh.astype(BF16)
        o.g_expand[...] += dot_tn(n2, dh)
        dn = dot_nn(dh, o.expand_t[...])
        o.g_small[2:3, :] += jnp.sum(dn * xhat, axis=0, keepdims=True)
        o.g_small[3:4, :] += jnp.sum(dn, axis=0, keepdims=True)
        dm = g + norm_pull(xhat, rstd, o.vecs[2:3, :], dn)
        o.grad[rows, :] = dm
        db = dm.astype(BF16)
        o.g_exit[...] += dot_tn(o.att[p, rows, :], db)
        o.datt[rows, :] = dot_nn(db, o.exit_t[...]).astype(BF16)

    def ff_first(rows):
        mid, xhat, rstd, n2, act, gp, res = feed_forward(0, rows)
        o.middle[rows, :] = mid
        o.active[rows, :] = act
        o.gelup[rows, :] = gp.astype(BF16)
        o.grad[rows, :] = res

    def ff_last(rows):
        mid, xhat, rstd, n2, act, gp, res = feed_forward(1, rows)
        o.final[rows, :] = res.astype(BF16)
        feed_backward(1, rows, o.grad_in[rows, :].astype(F32), xhat, rstd, n2, act, gp)

    def ff_back(rows):
        xhat, rstd = norm_parts(o.middle[rows, :])
        n2 = (xhat * o.vecs[2:3, :] + o.vecs[3:4, :]).astype(BF16)
        feed_backward(0, rows, o.grad[rows, :], xhat, rstd, n2, o.active[rows, :], o.gelup[rows, :].astype(F32))

    def leave(p):
        lg, ls = o.vecs[0:1, :], o.vecs[1:2, :]

        def fn(rows):
            xhat, rstd = norm_parts(o.mixed[p, rows, :])
            dqkv = o.qkv[p, rows, :]
            o.g_entry[...] += dot_tn((xhat * lg + ls).astype(BF16), dqkv)
            dn = dot_nn(dqkv, o.entry_t[...])
            o.g_small[0:1, :] += jnp.sum(dn * xhat, axis=0, keepdims=True)
            o.g_small[1:2, :] += jnp.sum(dn, axis=0, keepdims=True)
            g = o.grad[rows, :] + norm_pull(xhat, rstd, lg, dn)
            o.grad[rows, :] = g
            o.total[rows, :] = g if p == 1 else o.total[rows, :] + g
        tiles(RC, fn)

    def backward(p, hook=None):
        attn_backward(o.qkv, p, o.att, o.lx, o.datt, o.vx, o.kx, o.qx, o.dox, o.dk, o.dv, o.dq, seqs, hook)

    def clear():
        zero(o.g_entry, o.g_exit, o.g_expand, o.g_reduce_t, o.g_small, o.g_exp_b)

    if comm:
        links = Links(n)
        arrived = links.barrier()
        pack_parameters()
        arrived()
        links.gather_start(o.buf1, o.sem1, 0)
        clear()
        links.gather_wait(o.buf1, o.sem1, 0)
        links.gather_start(o.buf1, o.sem1, 1)
        links.gather_start(o.buf2, o.sem2, 0)
        links.gather_wait(o.buf1, o.sem1, 1)
        links.gather_start(o.buf1, o.sem1, 2)
        links.gather_wait(o.buf1, o.sem1, 2)
        unpack_first()
    else:
        clear()
        for i, r in enumerate((o.lead_g, o.lead_s, o.mid_g, o.mid_s, o.red_b)):
            o.vecs[i:i + 1, :] = r[...].astype(F32)
        o.eb[...] = o.exp_b[...].astype(F32)
        o.entry_t[...] = o.entry_w[...].T
        turn_second()

    enter(0)
    if comm:
        links.gather_wait(o.buf2, o.sem2, 0)
        links.gather_start(o.buf2, o.sem2, 1)

        def gather_more(it):
            @pl.when(it == seqs)
            def _():
                links.gather_wait(o.buf2, o.sem2, 1)
                links.gather_start(o.buf2, o.sem2, 2)

        attn_forward(o.qkv, 0, o.att, o.lx, o.vx, seqs, gather_more)
        links.gather_wait(o.buf2, o.sem2, 2)
        unpack_second()
    else:
        attn_forward(o.qkv, 0, o.att, o.lx, o.vx, seqs)
    tiles(RF, ff_first)
    enter(1)
    attn_forward(o.qkv, 1, o.att, o.lx, o.vx, seqs)
    tiles(RF, ff_last)
    backward(1)
    leave(1)
    tiles(RF, ff_back)
    if comm:
        feed_reduce_pack()
        links.reduce_start(o.buf2, o.feed_got0, o.sem3, 2)

        def reduce_more(it):
            @pl.when(it == 1)
            def _():
                o.feed_part1[...] = links.reduce_wait(o.buf2, o.feed_got0, o.sem3, 2).astype(BF16)
                links.reduce_start(o.feed_part1, o.feed_got1, o.sem3, 1)

            @pl.when(it == 2 * seqs - 2)
            def _():
                o.feed_part2[...] = links.reduce_wait(o.feed_part1, o.feed_got1, o.sem3, 1).astype(BF16)
                links.reduce_start(o.feed_part2, o.feed_got2, o.sem3, 0)

        backward(0, reduce_more)
        feed_reduce_end(links.reduce_wait(o.feed_part2, o.feed_got2, o.sem3, 0))
        leave(0)
        entry_reduce_pack()
        links.reduce_start(o.buf1, o.entry_got0, o.sem4, 2)
        o.entry_part1[...] = links.reduce_wait(o.buf1, o.entry_got0, o.sem4, 2).astype(BF16)
        links.reduce_start(o.entry_part1, o.entry_got1, o.sem4, 1)
        o.entry_part2[...] = links.reduce_wait(o.entry_part1, o.entry_got1, o.sem4, 1).astype(BF16)
        links.reduce_start(o.entry_part2, o.entry_got2, o.sem4, 0)
        entry_reduce_end(links.reduce_wait(o.entry_part2, o.entry_got2, o.sem4, 0))
    else:
        backward(0)
        leave(0)
        o.g_reduce[...] = o.g_reduce_t[...].T
        for i in range(4):
            o.g_small[8 + i:9 + i, :] = o.g_exp_b[:, i * D:(i + 1) * D]


TOKEN_INPUTS = ("state_in", "embed_in", "grad_in")
VECTOR_INPUTS = ("lead_g", "lead_s", "mid_g", "mid_s", "red_b", "exp_b")


def mega(n, tokens, comm):
    T = tokens
    sds, vmem = jax.ShapeDtypeStruct, pltpu.VMEM
    outs = [("final", sds((T, D), BF16)), ("grad", sds((T, D), F32)), ("total", sds((T, D), F32))]
    scratch = [
        ("mixed", vmem((2, T, D), F32)), ("qkv", vmem((2, T, 3 * D), BF16)), ("att", vmem((2, T, D), BF16)), ("lx", vmem((2, T, D), BF16)),
        ("middle", vmem((T, D), F32)), ("active", vmem((T, FF), BF16)), ("gelup", vmem((T, FF), BF16)), ("datt", vmem((T, D), BF16)),
        ("entry_t", vmem((3 * D, D), BF16)), ("exit_t", vmem((D, D), BF16)), ("expand_t", vmem((FF, D), BF16)), ("reduce_t", vmem((D, FF), BF16)),
        ("vecs", vmem((8, D), F32)), ("eb", vmem((1, FF), F32)),
        ("vx", vmem((2, LEN, 128), BF16)), ("kx", vmem((2, LEN, 128), BF16)), ("qx", vmem((2, LEN, 128), BF16)), ("dox", vmem((2, LEN, 128), BF16)),
        ("dk", vmem((2, LEN, 128), F32)), ("dv", vmem((2, LEN, 128), F32)), ("dq", vmem((2, LEN, 128), F32)),
        ("g_reduce_t", vmem((D, FF), F32)), ("g_exp_b", vmem((1, FF), F32)),
    ]
    grads = [("g_entry", (D, 3 * D)), ("g_exit", (D, D)), ("g_expand", (D, FF)), ("g_small", (16, D))]
    weights = [("entry_w", (D, 3 * D)), ("exit_w", (D, D)), ("expand_w", (D, FF)), ("reduce_w", (FF, D))]
    if comm:
        ins = TOKEN_INPUTS + ("entry_s", "exit_s", "expand_s", "reduce_s") + VECTOR_INPUTS
        r, rr = D // n, FF // n
        outs += [
            ("entry_o", sds((r, 3 * D), F32)), ("exit_o", sds((r, D), F32)), ("lead_g_o", sds((r,), F32)), ("lead_s_o", sds((r,), F32)),
            ("expand_o", sds((r, FF), F32)), ("reduce_o", sds((rr, D), F32)), ("mid_g_o", sds((r,), F32)), ("mid_s_o", sds((r,), F32)),
            ("exp_b_o", sds((rr,), F32)), ("red_b_o", sds((r,), F32)),
        ]
        scratch += [(name, vmem(shape, F32)) for name, shape in grads] + [(name, vmem(shape, BF16)) for name, shape in weights]
        s = tuple(size for _, size in digit_groups(n))
        scratch += [("vec", vmem((16, 128), F32))]
        scratch += [("buf1", vmem(s + (ENTRY_ROWS, 128), BF16)), ("buf2", vmem(s + (FEED_ROWS, 128), BF16))]
        for name, rows in (("entry", ENTRY_ROWS), ("feed", FEED_ROWS)):
            for step, g in enumerate((2, 1, 0)):
                scratch.append((f"{name}_got{step}", vmem((s[g] - 1,) + s[:g] + (rows, 128), BF16)))
                if g < 2:
                    scratch.append((f"{name}_part{step}", vmem(s[: g + 1] + (rows, 128), BF16)))
        scratch += [(f"sem{i}", pltpu.SemaphoreType.DMA((2, 3, 3))) for i in (1, 2, 3, 4)]
    else:
        ins = TOKEN_INPUTS + tuple(name for name, _ in weights) + VECTOR_INPUTS
        outs += [(name, sds(shape, F32)) for name, shape in grads] + [("g_reduce", sds((FF, D), F32))]
    names = ins + tuple(name for name, _ in outs) + tuple(name for name, _ in scratch)
    spec = pl.BlockSpec(memory_space=pltpu.VMEM)
    params = dict(collective_id=0, has_side_effects=True) if comm else {}
    return pl.pallas_call(
        functools.partial(mega_kernel, names=names, n=n, tokens=T, comm=comm),
        in_specs=[spec] * len(ins),
        out_specs=[spec] * len(outs),
        out_shape=[shape for _, shape in outs],
        scratch_shapes=[shape for _, shape in scratch],
        compiler_params=pltpu.CompilerParams(vmem_limit_bytes=62 * 1024 * 1024, **params),
        name="block",
    )


def on_device(loop_state, embedding, output_grad, entry_weight, exit_weight, lead_gain, lead_shift, expand_weight, reduce_weight, middle_gain, middle_shift, expand_bias, reduce_bias):
    n = lax.axis_size("fsdp")
    tokens = loop_state.shape[0]
    vectors = (lead_gain, lead_shift, middle_gain, middle_shift, reduce_bias, expand_bias)
    weights = (entry_weight, exit_weight, expand_weight, reduce_weight)
    if entry_weight.shape[0] == 8 and len(digit_groups(n)) == 3:
        final, grad, total, entry_g, exit_g, lgg, lsg, expand_g, reduce_g, mgg, msg, ebg, rbg = mega(n, tokens, True)(
            loop_state, embedding, output_grad, *weights, *vectors
        )
        return (final, grad, total, entry_g, exit_g, lgg, lsg, expand_g, reduce_g, mgg, msg, ebg, rbg)
    shards = weights + vectors
    packed = jnp.concatenate([a.reshape(-1) for a in shards])
    whole = lax.all_gather(packed, "fsdp", axis=0)
    full, at = [], 0
    for a in shards:
        whole_a = whole[:, at : at + a.size].reshape((n * a.shape[0],) + a.shape[1:])
        full.append(whole_a if a.ndim == 2 else whole_a.reshape(1, -1))
        at += a.size
    final, grad, total, g_entry, g_exit, g_expand, small, g_reduce = mega(n, tokens, False)(loop_state, embedding, output_grad, *full)
    terms = (g_entry, g_exit, small[0], small[1], g_expand, g_reduce, small[2], small[3], small[8:12].reshape(-1), small[5])
    sums = lax.psum_scatter(jnp.concatenate([a.reshape(n, -1) for a in terms], axis=1), "fsdp", scatter_dimension=0, tiled=True)[0]
    outs, at = [], 0
    for a in terms:
        size = a.size // n
        outs.append(sums[at : at + size].reshape((a.shape[0] // n,) + a.shape[1:]))
        at += size
    return (final, grad, total, *outs)


def solution(mesh):
    two, one = P("fsdp", None), P("fsdp")
    in_specs = (two, two, two, two, two, one, one, two, two, one, one, one, one)
    out_specs = (two, two, two, two, two, one, one, two, two, one, one, one, one)
    return jax.shard_map(on_device, mesh=mesh, in_specs=in_specs, out_specs=out_specs, check_vma=False)
```

time: 438 us -> 158 us (0.36)
  waiting for transfers between devices: 272 us -> 0 us
  Pallas kernels: 113 us -> 146 us
  local copies, waits for them, and re-layouts: 37.3 us -> 11.6 us
  between operations: 14.2 us -> 0.73 us
    unnamed x4 -> x0, waiting for transfers between devices: 272 us -> none
    pallas_call x1, Pallas kernels: 113 us -> 146 us  [on_device(): mega(n, tokens, True)]
    reshape x13 -> x0, local copies, waits for them, and re-layouts: 10.8 us -> none  [the longest x4 3.86 us: on_device(): a.reshape(n, -1)]
    slice x12 -> x0, local copies, waits for them, and re-layouts: 7.84 us -> none  [the longest x5 5.94 us: on_device(): outs.append(sums[at:at + size].reshape(shape))]
    unnamed x9 -> x37, local copies, waits for them, and re-layouts: 4 us -> 11.6 us
    concatenate x2 -> x0, local copies, waits for them, and re-layouts: 6.5 us -> none  [the longest x1 4.1 us: on_device(): packed = jnp.concatenate([a.reshape(-1) for a in shards])]
    another operation x12 -> x0, local copies, waits for them, and re-layouts: 4.49 us -> none  [the longest x6 3.99 us: on_device(): row = lambda a: a.reshape(1, -1)]
  transfers between devices with their start and end apart: 2 -> 0, of which waited for: 2 -> 0; matrix products, arithmetic and copies ran while one was open for 0% -> 0% of each run, Pallas kernels for 0% -> 0%
where the time goes in v2:
time: 158 us
  Pallas kernels  146 us (92%)
  local copies, waits for them, and re-layouts  11.6 us (7%)
    pallas_call x1, Pallas kernels, on_device(): mega(n, tokens, True)  146 us
    unnamed x37, local copies, waits for them, and re-layouts  11.6 us

profile of v2, /device:TPU:0, one launch (start us, length us, event | category | flops | bytes accessed | tf_op | source)
XLA Modules:
  0.0 158.0 jit_solution(11279976854255755388)
XLA Ops:
  0.6 145.7 %block.1 = (bf16[2048,256]{1,0:T(8,128)(2,1)}, f32[2048,256]{1,0:T(8,128)}, f32[2048,256]{1,0:T(8,128)}, f32[8,768]{1,0:T(8,128)}, f32[8,256]{1,0:T(8,128)}, /*i...) custom-call(bf16[2048,256]{1,0:T(8,128)(2,1)} %refs_0_.1, ...), custom_call_target="tpu_custom_call" | custom-call | tf_op jit(solution)/shard_map/block/pallas_call | solution.py:606
  146.3 0.0 copy-start.1
  146.3 2.4 %copy.39 = bf16[2048,256]{1,0:T(8,128)(2,1)} copy(bf16[2048,256]{1,0:T(8,128)(2,1)} %get-tuple-element.26) | data formatting | bytes 2097152
  148.8 0.0 copy-done.1
  148.8 1.3 copy.40
  150.1 1.0 copy-done
  151.1 0.0 copy-start.3
  151.1 0.0 copy-start.2
  151.1 0.0 copy-start.9
  151.1 0.0 copy-start.8
  151.2 0.0 copy-start.7
  151.2 0.0 copy-start.6
  151.2 1.3 copy.41
  152.5 0.0 copy-done.4
  152.5 0.6 copy.42
  153.1 0.0 copy-done.5
  153.1 0.6 copy.43
  153.7 0.0 copy-done.11
  153.7 0.5 copy.44
  154.2 0.0 copy-done.10
  154.2 0.5 copy.45
  154.7 0.0 copy-done.3
  154.7 0.6 copy.46
  155.4 0.0 copy-done.2
  155.4 0.6 copy.47
  156.0 0.0 copy-done.9
  156.0 0.5 copy.48
  156.5 0.0 copy-done.8
  156.5 0.5 copy.49
  157.0 0.5 copy.50
  157.5 0.0 copy-done.6
  157.5 0.5 copy.51
  (6 shorter events, 0.0 us)
Async XLA Ops:
  146.3 2.4 %copy-start.1 = (f32[2048,256]{1,0:T(8,128)S(1)}, f32[2048,256]{1,0:T(8,128)}, u32[]{:S(2)}) copy-start(f32[2048,256]{1,0:T(8,128)} %get-tuple-element.27) | copy-start | bytes 6291460
  148.8 2.3 %copy-start = (f32[2048,256]{1,0:T(8,128)S(1)}, f32[2048,256]{1,0:T(8,128)}, u32[]{:S(2)}) copy-start(f32[2048,256]{1,0:T(8,128)} %get-tuple-element.28) | copy-start | bytes 6291460
  151.1 1.4 copy-start.4
  151.1 2.0 %copy-start.5 = (f32[8,256]{1,0:T(8,128)S(1)}, f32[8,256]{1,0:T(8,128)}, u32[]{:S(2)}) copy-start(f32[8,256]{1,0:T(8,128)} %get-tuple-element.30) | copy-start | bytes 24580
  151.1 2.6 %copy-start.11 = (f32[8]{0:T(128)S(1)}, f32[8]{0:T(128)}, u32[]{:S(2)}) copy-start(f32[8]{0:T(128)} %get-tuple-element.31) | copy-start | bytes 100
  151.1 3.1 %copy-start.10 = (f32[8]{0:T(128)S(1)}, f32[8]{0:T(128)}, u32[]{:S(2)}) copy-start(f32[8]{0:T(128)} %get-tuple-element.32) | copy-start | bytes 100
  151.1 3.6 %copy-start.3 = (f32[8,1024]{1,0:T(8,128)S(1)}, f32[8,1024]{1,0:T(8,128)}, u32[]{:S(2)}) copy-start(f32[8,1024]{1,0:T(8,128)} %get-tuple-element.33) | copy-start | bytes 98308
  151.1 4.2 %copy-start.2 = (f32[32,256]{1,0:T(8,128)S(1)}, f32[32,256]{1,0:T(8,128)}, u32[]{:S(2)}) copy-start(f32[32,256]{1,0:T(8,128)} %get-tuple-element.34) | copy-start | bytes 98308
  151.1 4.8 %copy-start.9 = (f32[8]{0:T(128)S(1)}, f32[8]{0:T(128)}, u32[]{:S(2)}) copy-start(f32[8]{0:T(128)} %get-tuple-element.35) | copy-start | bytes 100
  151.1 5.3 %copy-start.8 = (f32[8]{0:T(128)S(1)}, f32[8]{0:T(128)}, u32[]{:S(2)}) copy-start(f32[8]{0:T(128)} %get-tuple-element.36) | copy-start | bytes 100
  151.2 5.9 %copy-start.7 = (f32[32]{0:T(128)S(1)}, f32[32]{0:T(128)}, u32[]{:S(2)}) copy-start(f32[32]{0:T(128)} %get-tuple-element.37) | copy-start | bytes 388
  151.2 6.4 %copy-start.6 = (f32[8]{0:T(128)S(1)}, f32[8]{0:T(128)}, u32[]{:S(2)}) copy-start(f32[8]{0:T(128)} %get-tuple-element.38) | copy-start | bytes 100
